TPU v7x, 256 devices: a whole 4x4x8 slice. The times are simulated.
256 devices in a mesh: dp: 4 (over x), gx: 8 (over y, z_lo), gy: 8 (over z_hi, core).
Axes of the slice: x: 4, y: 4, z: 8 (z_hi: 4, z_lo: 2; z = z_hi * 2 + z_lo), core: 2. Of those that a mesh axis runs over, the one named last changes fastest.
Arguments:
- field: float32 [4, 32, 64, 128, 128], P('dp', None, 'gx', 'gy'), may hold values from -6 to 6
- cotangent: float32 [4, 32, 64, 128, 128], P('dp', None, 'gx', 'gy'), may hold values from -6 to 6
- spectral_weight: float32 [512, 32768], P(('gx', 'gy'), 'dp'), may hold values from -1 to 1
- pointwise_weight: float32 [32, 32], replicated, may hold values from -1 to 1
- bias: float32 [32], replicated, may hold values from -3 to 3
Outputs:
- grad_input: float32 [4, 32, 64, 128, 128], P('dp', None, 'gx', 'gy')
- grad_spectral: float32 [512, 32768], P(('gx', 'gy'), 'dp')
All inputs are finite; a program needn't handle non-finite values.
Results may differ from a plain program's by a relative error of at most 0.00011.
Values sent between devices are 32-bit elements; how exact they have to be, the bound alone decides.
A program may use at most 128 MiB of HBM per device.

v0:
```python
import math

import jax
import jax.numpy as jnp
import numpy as np
from jax import lax
from jax.experimental import pallas as pl
from jax.experimental.pallas import tpu as pltpu
from jax.sharding import PartitionSpec as P

C = 32
MX = 16
MY = 32
MZ = 16
NX = 64
NY = 128
NZ = 128

F32 = jnp.float32
BF16 = jnp.bfloat16
MESH = pl.DeviceIdType.MESH

KX = np.array([4 * ((d // 2) % 4) + 2 * (d % 2) + d // 8 for d in range(16)])


def cos_sin(count, freqs):
    turns = np.mod(np.arange(count)[:, None] * freqs[None, :], count)
    theta = turns * (2.0 * math.pi / count)
    return np.cos(theta), np.sin(theta)


def halves(table):
    table = table.astype(np.float32)
    high = table.astype(jnp.bfloat16)
    low = (table - high.astype(np.float32)).astype(jnp.bfloat16)
    return [high, low]


def tables():
    eye8 = np.eye(8)
    cz, sz = cos_sin(NZ, np.arange(MZ))
    ztable = np.stack([cz, -sz], -1)
    cx, sx = cos_sin(NX, KX - MX // 2)
    cy, sy = cos_sin(NY, np.arange(MY) - MY // 2)

    def forward(c, s):
        return np.stack([np.stack([c, -s], -1), np.stack([s, c], -1)], -2)

    def inverse(c, s):
        return np.stack([np.stack([c, s], -1), np.stack([-s, c], -1)], -2)

    z_fwd = np.einsum("zkr,cd->czrkd", ztable, eye8).reshape(8 * NZ, 2 * MZ * 8)
    z_inv = np.ascontiguousarray(z_fwd.T)
    fx = forward(cx, sx).reshape(8, 8, 16, 2, 2)
    x_fwd = np.einsum("gxdrq,yw->dqygrxw", fx, eye8).reshape(256, 1024)
    ix = inverse(cx, sx).reshape(8, 8, 16, 2, 2)
    x_inv = np.einsum("gxdqr,yw->grxydqw", ix, eye8).reshape(1024, 256)
    fy = forward(cy, sy).reshape(16, 8, MY, 2, 2)
    y_fwd = np.einsum("dyjqp->pjdqy", fy).reshape(64, 256)
    iy = inverse(cy, sy).reshape(16, 8, MY, 2, 2)
    y_inv = np.einsum("dyjpr->drypj", iy).reshape(256, 64)

    use = np.zeros((128, 2, 2, C, 2), np.float32)
    for i in range(C):
        use[i, 0, :, i, 0] = 1.0
        use[C + i, 0, :, i, 1] = -1.0
        use[C + i, 1, :, i, 0] = 1.0
        use[i, 1, :, i, 1] = 1.0
    spread = np.zeros((128, 16, 2, 2, C, 2), np.float32)
    for b in range(2):
        for o in range(C):
            spread[b * C + o, o // 2, b, o % 2] = 1.0
    spread = spread.reshape(128, 4096)
    fold = np.zeros((2, 2, C, 2, 128), np.float32)
    for i in range(C):
        fold[0, :, i, 0, i] = 1.0
        fold[1, :, i, 1, i] = 1.0
        fold[1, :, i, 0, C + i] = 1.0
        fold[0, :, i, 1, C + i] = -1.0
    rows8 = np.repeat(np.eye(C), 8, axis=0)
    out = []
    for t in (z_fwd, x_fwd, y_fwd, y_inv, x_inv, z_inv):
        out += halves(t)
    out += [
        t.astype(jnp.bfloat16)
        for t in (
            use.reshape(128, 256),
            spread,
            np.ascontiguousarray(spread.T),
            fold.reshape(256, 128),
            rows8,
        )
    ]
    return out


TABLES = tables()


def gelu_slope(values):
    normal_cdf = 0.5 * (1.0 + lax.erf(values * math.sqrt(0.5)))
    return normal_cdf + values * jnp.exp(-0.5 * values * values) * (1.0 / math.sqrt(2.0 * math.pi))


def split(x):
    high = x.astype(BF16)
    return high, (x - high.astype(F32)).astype(BF16)


def dot(a, b):
    return jnp.dot(a, b, preferred_element_type=F32)


def left3(high, low, x):
    xh, xl = split(x)
    return dot(high, xh) + (dot(low, xh) + dot(high, xl))


def right3(x, high, low):
    xh, xl = split(x)
    return dot(xh, high) + (dot(xl, high) + dot(xh, low))


def right2(x, table):
    xh, xl = split(x)
    return dot(xh, table) + dot(xl, table)


def lanes_of(rows):
    return lax.broadcasted_iota(jnp.int32, (rows, 128), 1)


def roll(x, shift):
    shift = shift % 128
    return pltpu.roll(x, shift, axis=1) if shift else x


def swap_groups(blocks):
    lane = lanes_of(32)
    out = []
    for a in range(4):
        total = jnp.zeros((32, 128), F32)
        for b in range(4):
            keep = ((lane % 32) // 8 == b) & (lane < 64)
            total = total + jnp.where(keep, roll(blocks[b], (b - a) * 8), 0.0)
        out.append(total)
    return out


def pack_kz(v):
    lane = lanes_of(32)
    return [
        jnp.where(lane < 32, roll(v[:32], -kzg * 32), roll(v[32:], 32 - kzg * 32)) for kzg in range(4)
    ]


def unpack_kz(blocks):
    lane = lanes_of(32)
    parts = []
    for p in range(2):
        total = jnp.zeros((32, 128), F32)
        for kzg in range(4):
            total = total + jnp.where(lane // 32 == kzg, roll(blocks[kzg], (kzg - p) * 32), 0.0)
        parts.append(total)
    return jnp.concatenate(parts, axis=0)


def kernel(
    field_hbm,
    cot_hbm,
    weight_hbm,
    point_ref,
    bias_ref,
    *rest,
):
    n_tab = len(TABLES)
    tab_hbm = rest[:n_tab]
    gi_hbm, gs_hbm = rest[n_tab : n_tab + 2]
    scratch = rest[n_tab + 2 :]
    tab = scratch[:n_tab]
    (
        field,
        cot,
        weight,
        local,
        slope,
        grad,
        gspec,
        point_kron,
        use_ref,
        out1,
        recv1,
        out2,
        recv2,
        out3,
        recv3,
        out4,
        recv4,
        out5,
        recv5,
        out6,
        recv6,
        in_sem,
        tab_sem,
        done_sem,
        send_sem,
        recv_sem,
    ) = scratch[n_tab:]
    (zfh, zfl, xfh, xfl, yfh, yfl, yih, yil, xih, xil, zih, zil, use, spread, gather, fold, rows8) = tab

    s = lax.axis_index("dp")
    gx = lax.axis_index("gx")
    h = lax.axis_index("gy")
    yp = gx // 2
    zl = gx % 2
    place = 2 * h + zl
    scale_cells = 1.0 / math.sqrt(NX * NY * NZ)
    scale_modes = 1.0 / math.sqrt(MX * MY * MZ)

    def fetch(k):
        return pltpu.make_async_copy(tab_hbm[k], tab[k], tab_sem.at[k])

    inputs = [
        pltpu.make_async_copy(a, b, in_sem.at[k])
        for k, (a, b) in enumerate(((field_hbm, field), (weight_hbm, weight), (cot_hbm, cot)))
    ]
    fetch(0).start()
    fetch(1).start()
    inputs[0].start()
    for k in range(2, n_tab):
        fetch(k).start()
    inputs[1].start()
    inputs[2].start()

    def push(src, dst, stage, device):
        pltpu.make_async_remote_copy(
            src_ref=src,
            dst_ref=dst,
            send_sem=send_sem.at[stage],
            recv_sem=recv_sem.at[stage],
            device_id=device,
            device_id_type=MESH,
        ).start()

    def keep(src, dst, stage):
        pltpu.make_async_copy(src, dst, recv_sem.at[stage]).start()

    def arrived(buffer, stage):
        pltpu.make_async_copy(buffer, buffer, recv_sem.at[stage]).wait()

    def sent(buffer, stage):
        pltpu.make_async_copy(buffer, buffer, send_sem.at[stage]).wait()

    def over_gx(src, dst, stage, k):
        to = (gx + k) % 8
        push(src.at[to], dst.at[gx], stage, (s, to, h))

    def over_ring(src, dst, stage):
        def one(k, carry):
            to = (place + k) % 16
            push(src.at[to], dst.at[place], stage, (s, 2 * yp + to % 2, to // 2))
            return carry

        lax.fori_loop(1, 16, one, 0)
        keep(src.at[place], dst.at[place], stage)

    on_self = yp == h % 4

    def to_owner(src, dst, stage):
        first = s * 4 + h % 4

        def one(k, carry):
            to = (first + k) % 16
            push(src.at[to], dst.at[s * 4 + yp], stage, (to // 4, 2 * (h % 4) + zl, (h // 4) * 4 + to % 4))
            return carry

        lax.fori_loop(1, 16, one, 0)
        pl.when(on_self)(lambda: keep(src.at[first], dst.at[s * 4 + yp], stage))

        @pl.when(jnp.logical_not(on_self))
        def _():
            one(0, 0)

    def from_owner(src, dst, stage):
        first = s * 4 + yp

        def one(k, carry):
            to = (first + k) % 16
            push(src.at[to], dst.at[s * 4 + h % 4], stage, (to // 4, 2 * (to % 4) + zl, (h // 4) * 4 + yp))
            return carry

        lax.fori_loop(1, 16, one, 0)
        pl.when(on_self)(lambda: keep(src.at[first], dst.at[s * 4 + h % 4], stage))

        @pl.when(jnp.logical_not(on_self))
        def _():
            one(0, 0)

    def depth_forward(grid, cg, dst):
        total = jnp.zeros((128, 256), F32)
        for pair in range(4):
            block = jnp.concatenate(
                [grid[cg * 8 + pair * 2 + k].reshape(128, 128) for k in range(2)], axis=1
            )
            rows = pl.ds(pair * 256, 256)
            total = total + right3(block, zfh[rows], zfl[rows])
        total = total.reshape(8, 2, 8, 256)
        for yh in range(2):
            for r in range(2):
                dst[cg * 2 + yh, r] = total[:, yh, :, r * 128 : (r + 1) * 128]

    def send_group(src, dst, stage, k):
        cg = (yp + k) % 4
        if k == 0:
            other = gx + 1 - 2 * zl
            push(src.at[other], dst.at[gx], stage, (s, other, h))
            keep(src.at[gx], dst.at[gx], stage)
        else:
            for yh in range(2):
                to = 2 * cg + (zl + yh) % 2
                push(src.at[to], dst.at[gx], stage, (s, to, h))

    def x_forward(buf):
        return left3(xfh[...], xfl[...], buf[...].reshape(1024, 128))

    def middle_forward(first, scale):
        n = 0 if first else 1
        arrived(recv1.at[n], 6 * n)
        out2[n] = x_forward(recv1.at[n]).reshape(16, 16, 128)
        over_ring(out2.at[n], recv2.at[n], 6 * n + 1)
        arrived(recv2.at[n], 6 * n + 1)
        v = left3(yfh[...], yfl[...], recv2[n].reshape(256, 128)) * scale
        for kzg, block in enumerate(pack_kz(v)):
            out3[n, pl.ds(kzg * 4, 4)] = block.reshape(4, 8, 128)
        to_owner(out3.at[n], recv3.at[n], 6 * n + 2)

    def owner_rows(n):
        arrived(recv3.at[n], 6 * n + 2)
        value = recv3[n].reshape(4, 4, 8, 128)
        return jnp.concatenate(swap_groups([value[:, cg].reshape(32, 128) for cg in range(4)]), axis=0)

    def middle_inverse(rows, n, scale):
        blocks = swap_groups([rows[kz * 32 : (kz + 1) * 32] * scale for kz in range(4)])
        for cg in range(4):
            block = blocks[cg].reshape(4, 8, 128)
            for t in range(4):
                out4[n, t * 4 + cg] = block[t]
        from_owner(out4.at[n], recv4.at[n], 6 * n + 3)
        arrived(recv4.at[n], 6 * n + 3)
        value = recv4[n].reshape(4, 32, 128)
        planes = unpack_kz([value[kzg] for kzg in range(4)])
        out5[n] = left3(yih[...], yil[...], planes).reshape(16, 16, 128)
        over_ring(out5.at[n], recv5.at[n], 6 * n + 4)
        arrived(recv5.at[n], 6 * n + 4)
        rows5 = recv5[n].reshape(256, 128)
        high, low = split(rows5)
        for k in range(8):
            part = pl.ds(k * 128, 128)
            block = dot(xih[part], high) + (dot(xil[part], high) + dot(xih[part], low))
            out6[n, k] = block.reshape(2, 8, 8, 128)
        for k in range(1, 8):
            over_gx(out6.at[n], recv6.at[n], 6 * n + 5, k)
        keep(out6.at[n, gx], recv6.at[n, gx], 6 * n + 5)

    def depth_inverse(n, cg, finish):
        halves_ = []
        for yh in range(2):
            halves_.append(
                jnp.concatenate([recv6[n, cg * 2 + yh, r].reshape(64, 128) for r in range(2)], axis=1)
            )
        high, low = split(jnp.concatenate(halves_, axis=0))
        for pair in range(4):
            cols = pl.ds(pair * 256, 256)
            value = dot(high, zih[:, cols]) + (dot(low, zih[:, cols]) + dot(high, zil[:, cols]))
            for k in range(2):
                for yh in range(2):
                    finish(
                        cg * 8 + pair * 2 + k,
                        yh,
                        value[yh * 64 : (yh + 1) * 64, k * 128 : (k + 1) * 128].reshape(8, 8, 128),
                    )

    def kron(transposed):
        same = lax.broadcasted_iota(jnp.int32, (256, 256), 0) % 8 == (
            lax.broadcasted_iota(jnp.int32, (256, 256), 1) % 8
        )
        dims = (((1,), (1 if transposed else 0,)), ((), ()))
        for k, half in enumerate(split(point_ref[...])):
            tall = lax.dot_general(rows8[...], half, dims, preferred_element_type=F32).astype(BF16)
            wide = lax.dot_general(
                tall, rows8[...], (((1,), (1,)), ((), ())), preferred_element_type=F32
            )
            point_kron[k] = jnp.where(same, wide, 0.0).astype(BF16)

    def pointwise(src, dst):
        def one(x, carry):
            block = jnp.concatenate([src[:, x, yh].reshape(256, 128) for yh in range(2)], axis=1)
            value = left3(point_kron[0], point_kron[1], block)
            for yh in range(2):
                dst[:, x, yh] = value[:, yh * 128 : (yh + 1) * 128].reshape(32, 8, 128)
            return carry

        lax.fori_loop(0, 8, one, 0)

    fetch(0).wait()
    fetch(1).wait()
    inputs[0].wait()
    for k in (1, 2, 3, 0):
        depth_forward(field, (yp + k) % 4, out1.at[0])
        send_group(out1.at[0], recv1.at[0], 0, k)
    for k in range(2, n_tab):
        fetch(k).wait()
    kron(False)
    pointwise(field, local)
    middle_forward(True, scale_cells)

    inputs[1].wait()
    operands = right2(owner_rows(0), use[...])
    for b in range(2):
        use_ref[b] = operands[:, b * 128 : (b + 1) * 128].reshape(4, 4, 8, 128)

    def mix(pair, total):
        both = []
        for b in range(2):
            products = []
            for kz in range(4):
                cols = pl.ds(pl.multiple_of((kz * 16 + pair) * 128, 128), 128)
                products.append((use_ref[b, kz] * weight[:, cols][None]).reshape(32, 128))
            both.append(jnp.concatenate(products, axis=0))
        rows = pl.ds(pl.multiple_of(pair * 256, 256), 256)
        return total + right2(jnp.concatenate(both, axis=1), gather[rows])

    mixed = lax.fori_loop(0, 16, mix, jnp.zeros((128, 128), F32))
    middle_inverse(mixed, 0, scale_modes)

    inputs[2].wait()
    arrived(recv6.at[0], 5)

    def slope_of(c, yh, value):
        pre = value + local[c, :, yh] + bias_ref[c]
        slope[c, :, yh] = cot[c, :, yh] * gelu_slope(pre)

    for k in (1, 2, 3, 0):
        cg = (yp + k) % 4
        depth_inverse(0, cg, slope_of)
        depth_forward(slope, cg, out1.at[1])
        send_group(out1.at[1], recv1.at[1], 6, k)
    kron(True)
    pointwise(slope, local)
    middle_forward(False, scale_modes)

    spectra = owner_rows(1)
    spec_high, spec_low = split(spectra)

    def adjoint(pair, carry):
        first, second = carry
        cols = pl.ds(pl.multiple_of(pair * 256, 256), 256)
        wide = dot(spec_high, spread[:, cols]) + dot(spec_low, spread[:, cols])
        zr = wide[:, :128].reshape(4, 4, 8, 128)
        zi = wide[:, 128:].reshape(4, 4, 8, 128)
        ones, twos = [], []
        for kz in range(4):
            cols = pl.ds(pl.multiple_of((kz * 16 + pair) * 128, 128), 128)
            tile = weight[:, cols][None]
            ones.append(zr[kz] * tile)
            twos.append(zi[kz] * tile)
            gspec[:, cols] = jnp.sum(zr[kz] * use_ref[0, kz] + zi[kz] * use_ref[1, kz], axis=0)
        return first + jnp.stack(ones), second + jnp.stack(twos)

    zero = jnp.zeros((4, 4, 8, 128), F32)
    first, second = lax.fori_loop(0, 16, adjoint, (zero, zero))
    both = jnp.concatenate([first.reshape(128, 128), second.reshape(128, 128)], axis=1)
    spec_out = pltpu.make_async_copy(gspec, gs_hbm, done_sem.at[4])
    spec_out.start()
    middle_inverse(right2(both, fold[...]), 1, scale_cells)
    arrived(recv6.at[1], 11)

    def finish(c, yh, value):
        grad[c, :, yh] = value + local[c, :, yh]

    results = []
    for cg in range(4):
        depth_inverse(1, cg, finish)
        part = pl.ds(cg * 8, 8)
        results.append(pltpu.make_async_copy(grad.at[part], gi_hbm.at[part], done_sem.at[cg]))
        results[-1].start()

    for n in range(2):
        sent(out1.at[n, pl.ds(0, 7)], 6 * n)
        sent(out2.at[n, pl.ds(0, 15)], 6 * n + 1)
        sent(out5.at[n, pl.ds(0, 15)], 6 * n + 4)
        sent(out6.at[n, pl.ds(0, 7)], 6 * n + 5)
        for buf, stage in ((out3, 6 * n + 2), (out4, 6 * n + 3)):
            sent(buf.at[n, pl.ds(0, 15)], stage)
            pl.when(jnp.logical_not(on_self))(lambda buf=buf, stage=stage: sent(buf.at[n, 0], stage))
    spec_out.wait()
    for copy in results:
        copy.wait()


def body(field, cotangent, spectral_weight, pointwise_weight, bias):
    shape = (C, 8, 2, 8, NZ)
    big = (2, 8, 2, 8, 8, 128)
    ring = (2, 16, 16, 128)
    modes = (2, 16, 8, 128)
    any_spec = pl.BlockSpec(memory_space=pl.ANY)
    grad_input, grad_spectral = pl.pallas_call(
        kernel,
        out_shape=(
            jax.ShapeDtypeStruct(shape, F32),
            jax.ShapeDtypeStruct(spectral_weight.shape, F32),
        ),
        in_specs=[any_spec] * 3
        + [pl.BlockSpec(memory_space=pltpu.VMEM), pl.BlockSpec(memory_space=pltpu.SMEM)]
        + [any_spec] * len(TABLES),
        out_specs=(any_spec, any_spec),
        scratch_shapes=[pltpu.VMEM(t.shape, BF16) for t in TABLES]
        + [
            pltpu.VMEM(shape, F32),
            pltpu.VMEM(shape, F32),
            pltpu.VMEM((8, 8192), F32),
            pltpu.VMEM(shape, F32),
            pltpu.VMEM(shape, F32),
            pltpu.VMEM(shape, F32),
            pltpu.VMEM((8, 8192), F32),
            pltpu.VMEM((2, 256, 256), BF16),
            pltpu.VMEM((2, 4, 4, 8, 128), F32),
            pltpu.VMEM(big, F32),
            pltpu.VMEM(big, F32),
            pltpu.VMEM(ring, F32),
            pltpu.VMEM(ring, F32),
            pltpu.VMEM(modes, F32),
            pltpu.VMEM(modes, F32),
            pltpu.VMEM(modes, F32),
            pltpu.VMEM(modes, F32),
            pltpu.VMEM(ring, F32),
            pltpu.VMEM(ring, F32),
            pltpu.VMEM(big, F32),
            pltpu.VMEM(big, F32),
            pltpu.SemaphoreType.DMA((3,)),
            pltpu.SemaphoreType.DMA((len(TABLES),)),
            pltpu.SemaphoreType.DMA((5,)),
            pltpu.SemaphoreType.DMA((12,)),
            pltpu.SemaphoreType.DMA((12,)),
        ],
        compiler_params=pltpu.CompilerParams(
            has_side_effects=True, vmem_limit_bytes=48 * 1024 * 1024
        ),
        name="fno_backward",
    )(
        field.reshape(shape),
        cotangent.reshape(shape),
        spectral_weight,
        pointwise_weight,
        bias,
        *[jnp.asarray(t) for t in TABLES],
    )
    return grad_input.reshape(field.shape), grad_spectral


def solution(mesh):
    placed = (
        P("dp", None, "gx", "gy", None),
        P("dp", None, "gx", "gy", None),
        P(("gx", "gy"), "dp"),
        P(),
        P(),
    )
    return jax.shard_map(
        body,
        mesh=mesh,
        in_specs=placed,
        out_specs=(P("dp", None, "gx", "gy", None), P(("gx", "gy"), "dp")),
        check_vma=False,
    )
```

profile of v0, /device:TPU:1, one launch (start us, length us, event | category | flops | bytes accessed | tf_op | source)
XLA Modules:
  0.0 137.7 jit_solution(10226207166620102358)
XLA Ops:
  0.6 0.0 copy-start
  0.6 1.2 copy-done
  1.9 0.0 copy-start.1
  1.9 1.0 copy-done.1
  2.9 1.0 copy-done.2
  3.9 1.0 copy-done.3
  5.0 1.0 copy-done.4
  6.0 1.0 copy-done.5
  7.1 1.0 copy-done.6
  8.1 1.0 copy-done.7
  9.2 1.0 copy-done.8
  10.2 0.9 copy-done.9
  11.1 0.8 copy-done.10
  12.0 0.8 copy-done.11
  12.8 0.8 copy-done.12
  13.7 0.8 copy-done.13
  14.5 0.8 copy-done.14
  15.3 0.8 copy-done.15
  16.1 0.8 copy-done.16
  16.9 0.7 copy-done.17
  17.6 0.7 copy-done.18
  18.2 115.7 %fno_backward.1 = (f32[32,8,2,8,128]{4,3,2,1,0:T(8,128)}, f32[8,8192]{1,0:T(8,128)S(1)}) custom-call(f32[32,8,2,8,128]{4,3,2,1,0:T(8,128)} %bitcast.4, f32[32,8,2,8,128]{4,3,2,1,0:T(8,128)} %bitcast.5, f32[8,8192]{1,0:T(8,128)S(1)} %copy-done.9, f32[32,32]{1,0:T(8,128)S(1)} %copy-done.17, f32[32]{0:T(128)S(1)} %copy-done.18, ...), custom_call_target="tpu_custom_call" | custom-call | tf_op jit(solution)/shard_map/fno_backward/pallas_call | solution.py:507
  133.9 3.1 %copy.26 = f32[1,32,8,16,128]{4,3,2,1,0:T(8,128)} copy(f32[1,32,8,16,128]{4,3,2,1,0:T(8,128)} %bitcast.3) | data formatting | bytes 4194304
  137.0 0.7 copy.27
  (17 shorter events, 0.0 us)
Async XLA Ops:
  0.6 1.2 copy-start
  1.9 1.0 copy-start.1
  2.9 1.0 copy-start.2
  3.9 1.0 copy-start.3
  5.0 1.0 copy-start.4
  6.0 1.0 copy-start.5
  7.1 1.0 copy-start.6
  8.1 1.0 copy-start.7
  9.2 1.0 copy-start.8
  10.2 0.9 copy-start.9
  11.1 0.8 copy-start.10
  12.0 0.8 copy-start.11
  12.8 0.8 copy-start.12
  13.7 0.8 copy-start.13
  14.5 0.8 copy-start.14
  15.3 0.8 copy-start.15
  16.1 0.8 copy-start.16
  16.9 0.7 copy-start.17
  17.6 0.7 copy-start.18
where the time goes:
time: 139 us; the launch traced here: 138 us
  Pallas kernels  116 us (83%)
  local copies, waits for them, and re-layouts  21.4 us (15%)
    pallas_call x1, Pallas kernels, body(): pl.pallas_call(kernel, out_shape=(jax.ShapeDtypeStruct(shape, F32), jax.S...  116 us
    unnamed x40, local copies, waits for them, and re-layouts  21.4 us

commit v1 on v0

v1 whole, which is shorter than its diff:
```python
import math

import jax
import jax.numpy as jnp
import numpy as np
from jax import lax
from jax.experimental import pallas as pl
from jax.experimental.pallas import tpu as pltpu
from jax.sharding import PartitionSpec as P

C = 32
MX = 16
MY = 32
MZ = 16
NX = 64
NY = 128
NZ = 128

F32 = jnp.float32
BF16 = jnp.bfloat16
MESH = pl.DeviceIdType.MESH

KX = np.array([4 * ((d // 2) % 4) + 2 * (d % 2) + d // 8 for d in range(16)])


def cos_sin(count, freqs):
    turns = np.mod(np.arange(count)[:, None] * freqs[None, :], count)
    theta = turns * (2.0 * math.pi / count)
    return np.cos(theta), np.sin(theta)


def halves(table):
    table = table.astype(np.float32)
    high = table.astype(jnp.bfloat16)
    low = (table - high.astype(np.float32)).astype(jnp.bfloat16)
    return [high, low]


def tables():
    eye8 = np.eye(8)
    cz, sz = cos_sin(NZ, np.arange(MZ))
    ztable = np.stack([cz, -sz], -1)
    cx, sx = cos_sin(NX, KX - MX // 2)
    cy, sy = cos_sin(NY, np.arange(MY) - MY // 2)

    def forward(c, s):
        return np.stack([np.stack([c, -s], -1), np.stack([s, c], -1)], -2)

    def inverse(c, s):
        return np.stack([np.stack([c, s], -1), np.stack([-s, c], -1)], -2)

    z_fwd = np.einsum("zkr,cd->czrkd", ztable, eye8).reshape(8 * NZ, 2 * MZ * 8)
    z_inv = np.ascontiguousarray(z_fwd.T)
    fx = forward(cx, sx).reshape(8, 8, 16, 2, 2)
    fx = fx.reshape(4, 2, 8, 16, 2, 2)
    x_fwd = np.einsum("gzxdrq,yw->zdqygrxw", fx, eye8).reshape(2, 256, 512)
    ix = inverse(cx, sx).reshape(8, 8, 16, 2, 2)
    ix = ix.reshape(4, 2, 8, 16, 2, 2)
    x_inv = np.einsum("gzxdqr,yw->zgrxydqw", ix, eye8).reshape(8, 128, 256)
    fy = forward(cy, sy).reshape(16, 8, MY, 2, 2)
    y_fwd = np.einsum("dyjqp->pjdqy", fy).reshape(64, 256)
    iy = inverse(cy, sy).reshape(16, 8, MY, 2, 2)
    y_inv = np.einsum("dyjpr->drypj", iy).reshape(256, 64)

    use = np.zeros((128, 2, 2, C, 2), np.float32)
    for i in range(C):
        use[i, 0, :, i, 0] = 1.0
        use[C + i, 0, :, i, 1] = -1.0
        use[C + i, 1, :, i, 0] = 1.0
        use[i, 1, :, i, 1] = 1.0
    spread = np.zeros((128, 16, 2, 2, C, 2), np.float32)
    for b in range(2):
        for o in range(C):
            spread[b * C + o, o // 2, b, o % 2] = 1.0
    spread = spread.reshape(128, 4096)
    fold = np.zeros((2, 2, C, 2, 128), np.float32)
    for i in range(C):
        fold[0, :, i, 0, i] = 1.0
        fold[1, :, i, 1, i] = 1.0
        fold[1, :, i, 0, C + i] = 1.0
        fold[0, :, i, 1, C + i] = -1.0
    rows8 = np.repeat(np.eye(C), 8, axis=0)
    out = []
    for t in (z_fwd, x_fwd, y_fwd, y_inv, x_inv, z_inv):
        out += halves(t)
    out += [
        t.astype(jnp.bfloat16)
        for t in (
            use.reshape(128, 256),
            spread,
            np.ascontiguousarray(spread.T),
            fold.reshape(256, 128),
            rows8,
        )
    ]
    return out


TABLES = tables()


def gelu_slope(values):
    normal_cdf = 0.5 * (1.0 + lax.erf(values * math.sqrt(0.5)))
    return normal_cdf + values * jnp.exp(-0.5 * values * values) * (1.0 / math.sqrt(2.0 * math.pi))


def split(x):
    high = x.astype(BF16)
    return high, (x - high.astype(F32)).astype(BF16)


def dot(a, b):
    return jnp.dot(a, b, preferred_element_type=F32)


def left3(high, low, x):
    xh, xl = split(x)
    return dot(high, xh) + (dot(low, xh) + dot(high, xl))


def right3(x, high, low):
    xh, xl = split(x)
    return dot(xh, high) + (dot(xl, high) + dot(xh, low))


def right2(x, table):
    xh, xl = split(x)
    return dot(xh, table) + dot(xl, table)


def lanes_of(rows):
    return lax.broadcasted_iota(jnp.int32, (rows, 128), 1)


def roll(x, shift):
    shift = shift % 128
    return pltpu.roll(x, shift, axis=1) if shift else x


def swap_groups(blocks):
    group = (lanes_of(64) % 32) // 8
    out = []
    for a in range(4):
        total = blocks[a]
        for b in range(4):
            if b != a:
                total = jnp.where(group == b, roll(blocks[b], (b - a) * 8), total)
        out.append(total)
    return out


def pack_kz(v):
    lane = lanes_of(32)
    return [
        jnp.where(lane < 32, roll(v[:32], -j * 32), roll(v[32:], 32 - j * 32)) for j in range(4)
    ]


def unpack_kz(blocks):
    lane = lanes_of(32)
    parts = []
    for p in range(2):
        total = jnp.zeros((32, 128), F32)
        for j in range(4):
            total = total + jnp.where(lane // 32 == j, roll(blocks[j], (j - p) * 32), 0.0)
        parts.append(total)
    return jnp.concatenate(parts, axis=0)


def kernel(
    field_hbm,
    cot_hbm,
    weight_hbm,
    point_ref,
    bias_ref,
    *rest,
):
    n_tab = len(TABLES)
    tab_hbm = rest[:n_tab]
    gi_hbm, gs_hbm = rest[n_tab : n_tab + 2]
    scratch = rest[n_tab + 2 :]
    tab = scratch[:n_tab]
    (
        field,
        cot,
        weight,
        local,
        slope,
        grad,
        gspec,
        wloc,
        gloc,
        grecv,
        gsum,
        point_kron,
        use_ref,
        out1,
        recv1,
        out2,
        recv2,
        out5,
        recv5,
        out6,
        recv6,
        in_sem,
        tab_sem,
        done_sem,
        send_sem,
        recv_sem,
    ) = scratch[n_tab:]
    (zfh, zfl, xfh, xfl, yfh, yfl, yih, yil, xih, xil, zih, zil, use, spread, gather, fold, rows8) = tab

    s = lax.axis_index("dp")
    gx = lax.axis_index("gx")
    h = lax.axis_index("gy")
    yp = gx // 2
    zl = gx % 2
    place = 2 * h + zl
    on_self = yp == h % 4
    scale_cells = 1.0 / math.sqrt(NX * NY * NZ)
    scale_modes = 1.0 / math.sqrt(MX * MY * MZ)

    def mover(k):
        return (s, 2 * k + zl, (h // 4) * 4 + yp)

    def owner(k):
        return (s, 2 * (h % 4) + zl, (h // 4) * 4 + k)

    barrier = pltpu.get_barrier_semaphore()

    def hello(device):
        pl.semaphore_signal(barrier, inc=1, device_id=device, device_id_type=MESH)

    for k in range(1, 16):
        to = (place + k) % 16
        hello((s, 2 * yp + to % 2, to // 2))
    for k in range(1, 8):
        hello((s, (gx + k) % 8, h))
    for k in range(1, 4):
        hello(((s + k) % 4, gx, h))
        hello(mover((yp + k) % 4))
        hello(owner((h + k) % 4))

    @pl.when(jnp.logical_not(on_self))
    def _():
        hello(mover(yp))
        hello(owner(h % 4))

    def fetch(k):
        return pltpu.make_async_copy(tab_hbm[k], tab[k], tab_sem.at[k])

    inputs = [
        pltpu.make_async_copy(a, b, in_sem.at[k])
        for k, (a, b) in enumerate(((field_hbm, field), (weight_hbm, weight), (cot_hbm, cot)))
    ]
    fetch(0).start()
    fetch(1).start()
    inputs[0].start()
    inputs[1].start()
    for k in range(2, n_tab):
        fetch(k).start()
    inputs[2].start()

    def push(src, dst, out_sem, in_sem, device):
        pltpu.make_async_remote_copy(
            src_ref=src,
            dst_ref=dst,
            send_sem=send_sem.at[out_sem],
            recv_sem=recv_sem.at[in_sem],
            device_id=device,
            device_id_type=MESH,
        ).start()

    def keep(src, dst, in_sem):
        pltpu.make_async_copy(src, dst, recv_sem.at[in_sem]).start()

    def arrived(buffer, in_sem):
        pltpu.make_async_copy(buffer, buffer, recv_sem.at[in_sem]).wait()

    def sent(buffer, out_sem):
        pltpu.make_async_copy(buffer, buffer, send_sem.at[out_sem]).wait()

    def send_gx(src, dst, stage, to_zl, dy):
        to_yp = (yp + dy) % 4
        block = to_zl * 4 + to_yp
        push(src.at[block], dst.at[zl * 4 + yp], stage, stage + zl, (s, 2 * to_yp + to_zl, h))

    def keep_gx(src, dst, stage):
        block = zl * 4 + yp
        keep(src.at[block], dst.at[block], stage + zl)

    def over_ring(src, dst, stage):
        for k in (8, 7, 9, 6, 10, 5, 11, 4, 12, 3, 13, 2, 14, 1, 15):
            to = (place + k) % 16
            push(src.at[to], dst.at[place], stage, stage, (s, 2 * yp + to % 2, to // 2))
        keep(src.at[place], dst.at[place], stage)

    def depth_forward(grid, half, dst):
        total = jnp.zeros((256, 256), F32)
        for pair in range(4):
            block = jnp.concatenate(
                [
                    jnp.concatenate(
                        [grid[cg * 8 + pair * 2 + k, :, half].reshape(64, 128) for k in range(2)], axis=1
                    )
                    for cg in range(4)
                ],
                axis=0,
            )
            rows = pl.ds(pair * 256, 256)
            total = total + right3(block, zfh[rows], zfl[rows])
        for r in range(2):
            blocks = [total[cg * 64 : (cg + 1) * 64, r * 128 : (r + 1) * 128] for cg in range(4)]
            for k, block in enumerate(swap_groups(blocks)):
                dst[half * 4 + k, r] = block.reshape(8, 8, 128)

    def send_half(n, half_is_own):
        half = zl if half_is_own else 1 - zl
        for dy in (2, 1, 3):
            send_gx(out1.at[n], recv1.at[n], 6 * n, half, dy)
        if half_is_own:
            keep_gx(out1.at[n], recv1.at[n], 6 * n)
        else:
            send_gx(out1.at[n], recv1.at[n], 6 * n, half, 0)

    def middle_forward(n, scale):
        total = None
        for half in (zl, 1 - zl):
            part = recv1.at[n, pl.ds(half * 4, 4)]
            arrived(part, 6 * n + half)
            term = left3(xfh[half], xfl[half], part[...].reshape(512, 128))
            total = term if total is None else total + term
        out2[n] = total.reshape(16, 16, 128)
        over_ring(out2.at[n], recv2.at[n], 6 * n + 2)
        if n == 0:
            spread_weights()
        arrived(recv2.at[n], 6 * n + 2)
        v = left3(yfh[...], yfl[...], recv2[n].reshape(256, 128)) * scale
        return jnp.concatenate(pack_kz(v), axis=0)

    def send_back(rows, n, scale):
        planes = unpack_kz([rows[j * 32 : (j + 1) * 32] * scale for j in range(4)])
        out5[n] = left3(yih[...], yil[...], planes).reshape(16, 16, 128)
        over_ring(out5.at[n], recv5.at[n], 6 * n + 3)

    def middle_inverse(n):
        arrived(recv5.at[n], 6 * n + 3)
        high, low = split(recv5[n].reshape(256, 128))
        for half_is_own in (False, True):
            half = zl if half_is_own else 1 - zl
            for dy in (2, 1, 3, 0):
                block = half * 4 + (yp + dy) % 4
                value = dot(xih[block], high) + (dot(xil[block], high) + dot(xih[block], low))
                out6[n, block] = value.reshape(2, 8, 8, 128)
                if half_is_own and dy == 0:
                    keep_gx(out6.at[n], recv6.at[n], 6 * n + 4)
                else:
                    send_gx(out6.at[n], recv6.at[n], 6 * n + 4, half, dy)

    def depth_inverse(n, half, finish):
        arrived(recv6.at[n, pl.ds(half * 4, 4)], 6 * n + 4 + half)
        parts = []
        for r in range(2):
            parts.append(swap_groups([recv6[n, half * 4 + k, r].reshape(64, 128) for k in range(4)]))
        rows = jnp.concatenate(
            [jnp.concatenate([parts[0][cg], parts[1][cg]], axis=1) for cg in range(4)], axis=0
        )
        high, low = split(rows)
        for pair in range(4):
            cols = pl.ds(pair * 256, 256)
            value = dot(high, zih[:, cols]) + (dot(low, zih[:, cols]) + dot(high, zil[:, cols]))
            for cg in range(4):
                for k in range(2):
                    finish(
                        cg * 8 + pair * 2 + k,
                        half,
                        value[cg * 64 : (cg + 1) * 64, k * 128 : (k + 1) * 128].reshape(8, 8, 128),
                    )

    def kron(transposed):
        same = lax.broadcasted_iota(jnp.int32, (256, 256), 0) % 8 == (
            lax.broadcasted_iota(jnp.int32, (256, 256), 1) % 8
        )
        dims = (((1,), (1 if transposed else 0,)), ((), ()))
        for k, half in enumerate(split(point_ref[...])):
            tall = lax.dot_general(rows8[...], half, dims, preferred_element_type=F32).astype(BF16)
            wide = lax.dot_general(
                tall, rows8[...], (((1,), (1,)), ((), ())), preferred_element_type=F32
            )
            point_kron[k] = jnp.where(same, wide, 0.0).astype(BF16)

    def pointwise(src, dst):
        def one(x, carry):
            block = jnp.concatenate([src[:, x, yh].reshape(256, 128) for yh in range(2)], axis=1)
            value = left3(point_kron[0], point_kron[1], block)
            for yh in range(2):
                dst[:, x, yh] = value[:, yh * 128 : (yh + 1) * 128].reshape(32, 8, 128)
            return carry

        lax.fori_loop(0, 8, one, 0)

    def weight_cols(k):
        return pl.ds(pl.multiple_of(k * 2048, 2048), 2048)

    def move_weights():
        inputs[1].wait()

        def one(k):
            push(weight.at[:, weight_cols(k)], wloc.at[s, h % 4], 12, 12, mover(k))

        for k in range(1, 4):
            one((yp + k) % 4)
        pl.when(on_self)(lambda: keep(weight.at[:, weight_cols(yp)], wloc.at[s, h % 4], 12))
        pl.when(jnp.logical_not(on_self))(lambda: one(yp))

    def spread_weights():
        arrived(wloc.at[s], 12)
        for k in (2, 1, 3):
            push(wloc.at[s], wloc.at[s], 13, 13, ((s + k) % 4, gx, h))

    def wait_weights():
        arrived(wloc.at[pl.ds(0, 3)], 13)

    fetch(0).wait()
    fetch(1).wait()
    inputs[0].wait()
    depth_forward(field, 1 - zl, out1.at[0])
    pl.when(on_self)(lambda: pl.semaphore_wait(barrier, 31))
    pl.when(jnp.logical_not(on_self))(lambda: pl.semaphore_wait(barrier, 33))
    send_half(0, False)
    depth_forward(field, zl, out1.at[0])
    send_half(0, True)
    move_weights()
    for k in range(2, n_tab):
        fetch(k).wait()
    kron(False)
    pointwise(field, local)

    operands = right2(middle_forward(0, scale_cells), use[...])
    for b in range(2):
        use_ref[b] = operands[:, b * 128 : (b + 1) * 128].reshape(4, 32, 128)
    wait_weights()

    def mix(pair, total):
        cols = pl.ds(pl.multiple_of(pair * 128, 128), 128)
        tiles = [wloc[j, :, :, cols].reshape(32, 128) for j in range(4)]
        both = [
            jnp.concatenate([use_ref[b, j] * tiles[j] for j in range(4)], axis=0) for b in range(2)
        ]
        rows = pl.ds(pl.multiple_of(pair * 256, 256), 256)
        return total + right2(jnp.concatenate(both, axis=1), gather[rows])

    mixed = lax.fori_loop(0, 16, mix, jnp.zeros((128, 128), F32))
    send_back(mixed, 0, scale_modes)
    middle_inverse(0)

    inputs[2].wait()

    def slope_of(c, half, value):
        pre = value + local[c, :, half] + bias_ref[c]
        slope[c, :, half] = cot[c, :, half] * gelu_slope(pre)

    for half_is_own in (True, False):
        half = zl if half_is_own else 1 - zl
        depth_inverse(0, half, slope_of)
        depth_forward(slope, half, out1.at[1])
        send_half(1, half_is_own)
    kron(True)
    pointwise(slope, local)

    spec_high, spec_low = split(middle_forward(1, scale_modes))

    def adjoint(pair, carry):
        first, second = carry
        cols = pl.ds(pl.multiple_of(pair * 256, 256), 256)
        wide = dot(spec_high, spread[:, cols]) + dot(spec_low, spread[:, cols])
        cols = pl.ds(pl.multiple_of(pair * 128, 128), 128)
        ones, twos = [], []
        for j in range(4):
            zr = wide[j * 32 : (j + 1) * 32, :128]
            zi = wide[j * 32 : (j + 1) * 32, 128:]
            tile = wloc[j, :, :, cols].reshape(32, 128)
            ones.append(zr * tile)
            twos.append(zi * tile)
            gloc[j, :, :, cols] = (zr * use_ref[0, j] + zi * use_ref[1, j]).reshape(4, 8, 128)
        return first + jnp.concatenate(ones, axis=0), second + jnp.concatenate(twos, axis=0)

    zero = jnp.zeros((128, 128), F32)
    both = jnp.concatenate(lax.fori_loop(0, 16, adjoint, (zero, zero)), axis=1)
    send_back(right2(both, fold[...]), 1, scale_cells)
    for k in (2, 1, 3):
        to = (s + k) % 4
        push(gloc.at[to], grecv.at[k - 1], 14, 14, (to, gx, h))
    middle_inverse(1)

    arrived(grecv, 14)
    for k in range(4):
        gsum[k] = (gloc[s, k] + grecv[0, k]) + (grecv[1, k] + grecv[2, k])

    def return_sum(k):
        push(gsum.at[k], gspec.at[:, weight_cols(yp)], 15, 15, owner(k))

    for k in range(1, 4):
        return_sum((h + k) % 4)
    pl.when(on_self)(lambda: keep(gsum.at[h % 4], gspec.at[:, weight_cols(yp)], 15))
    pl.when(jnp.logical_not(on_self))(lambda: return_sum(h % 4))

    def finish(c, half, value):
        grad[c, :, half] = value + local[c, :, half]

    depth_inverse(1, zl, finish)
    depth_inverse(1, 1 - zl, finish)
    grad_out = pltpu.make_async_copy(grad, gi_hbm, done_sem.at[0])
    grad_out.start()
    arrived(gspec, 15)
    spec_out = pltpu.make_async_copy(gspec, gs_hbm, done_sem.at[1])
    spec_out.start()

    for n in range(2):
        sent(out1.at[n, pl.ds(0, 7)], 6 * n)
        sent(out2.at[n, pl.ds(0, 15)], 6 * n + 2)
        sent(out5.at[n, pl.ds(0, 15)], 6 * n + 3)
        sent(out6.at[n, pl.ds(0, 7)], 6 * n + 4)
    sent(wloc.at[pl.ds(0, 3)], 13)
    sent(gloc.at[pl.ds(0, 3)], 14)
    sent(weight.at[:, pl.ds(0, 6144)], 12)
    sent(gsum.at[pl.ds(0, 3)], 15)

    @pl.when(jnp.logical_not(on_self))
    def _():
        sent(weight.at[:, pl.ds(0, 2048)], 12)
        sent(gsum.at[0], 15)

    grad_out.wait()
    spec_out.wait()


def body(field, cotangent, spectral_weight, pointwise_weight, bias):
    shape = (C, 8, 2, 8, NZ)
    big = (2, 8, 2, 8, 8, 128)
    ring = (2, 16, 16, 128)
    rows = (4, 4, 8, 2048)
    any_spec = pl.BlockSpec(memory_space=pl.ANY)
    grad_input, grad_spectral = pl.pallas_call(
        kernel,
        out_shape=(
            jax.ShapeDtypeStruct(shape, F32),
            jax.ShapeDtypeStruct(spectral_weight.shape, F32),
        ),
        in_specs=[any_spec] * 3
        + [pl.BlockSpec(memory_space=pltpu.VMEM), pl.BlockSpec(memory_space=pltpu.SMEM)]
        + [any_spec] * len(TABLES),
        out_specs=(any_spec, any_spec),
        scratch_shapes=[pltpu.VMEM(t.shape, BF16) for t in TABLES]
        + [
            pltpu.VMEM(shape, F32),
            pltpu.VMEM(shape, F32),
            pltpu.VMEM((8, 8192), F32),
            pltpu.VMEM(shape, F32),
            pltpu.VMEM(shape, F32),
            pltpu.VMEM(shape, F32),
            pltpu.VMEM((8, 8192), F32),
            pltpu.VMEM(rows, F32),
            pltpu.VMEM(rows, F32),
            pltpu.VMEM((3,) + rows[1:], F32),
            pltpu.VMEM(rows[1:], F32),
            pltpu.VMEM((2, 256, 256), BF16),
            pltpu.VMEM((2, 4, 32, 128), F32),
            pltpu.VMEM(big, F32),
            pltpu.VMEM(big, F32),
            pltpu.VMEM(ring, F32),
            pltpu.VMEM(ring, F32),
            pltpu.VMEM(ring, F32),
            pltpu.VMEM(ring, F32),
            pltpu.VMEM(big, F32),
            pltpu.VMEM(big, F32),
            pltpu.SemaphoreType.DMA((3,)),
            pltpu.SemaphoreType.DMA((len(TABLES),)),
            pltpu.SemaphoreType.DMA((2,)),
            pltpu.SemaphoreType.DMA((16,)),
            pltpu.SemaphoreType.DMA((16,)),
        ],
        compiler_params=pltpu.CompilerParams(
            has_side_effects=True, collective_id=0, vmem_limit_bytes=63 * 1024 * 1024
        ),
        name="fno_backward",
    )(
        field.reshape(shape),
        cotangent.reshape(shape),
        spectral_weight,
        pointwise_weight,
        bias,
        *[jnp.asarray(t) for t in TABLES],
    )
    return grad_input.reshape(field.shape), grad_spectral


def solution(mesh):
    placed = (
        P("dp", None, "gx", "gy", None),
        P("dp", None, "gx", "gy", None),
        P(("gx", "gy"), "dp"),
        P(),
        P(),
    )
    return jax.shard_map(
        body,
        mesh=mesh,
        in_specs=placed,
        out_specs=(P("dp", None, "gx", "gy", None), P(("gx", "gy"), "dp")),
        check_vma=False,
    )
```

time: 139 us -> 103 us (0.74)
  Pallas kernels: 116 us -> 97.4 us
  local copies, waits for them, and re-layouts: 21.4 us -> 3.88 us
    pallas_call x1, Pallas kernels: 116 us -> 97.4 us  [body(): pl.pallas_call(kernel, out_shape=(jax.ShapeDtypeStruct(shape, F32), jax.S...]
    unnamed x40 -> x4, local copies, waits for them, and re-layouts: 21.4 us -> 3.88 us
where the time goes in v1:
time: 103 us; the launch traced here: 102 us
  Pallas kernels  97.4 us (95%)
  local copies, waits for them, and re-layouts  3.88 us (4%)
    pallas_call x1, Pallas kernels, body(): pl.pallas_call(kernel, out_shape=(jax.ShapeDtypeStruct(shape, F32), jax.S...  97.4 us
    unnamed x4, local copies, waits for them, and re-layouts  3.88 us

profile of v1, /device:TPU:1, one launch (start us, length us, event | category | flops | bytes accessed | tf_op | source)
XLA Modules:
  0.0 102.0 jit_solution(6349346257172810960)
XLA Ops:
  0.6 97.4 %fno_backward.1 = (f32[32,8,2,8,128]{4,3,2,1,0:T(8,128)}, f32[8,8192]{1,0:T(8,128)}) custom-call(f32[32,8,2,8,128]{4,3,2,1,0:T(8,128)} %bitcast.4, f32[32,8,2,8,128]{4,3,2,1,0:T(8,128)} %bitcast.5, f32[8,8192]{1,0:T(8,128)} %weight_hbm.1, f32[32,32]{1,0:T(8,128)} %point_ref.1, f32[32]{0:T(128)} %bias_ref.1, bf16[1024,256]{1,0:T(8,128)(2,1)} %constant.34.clone.rest_0_, ...), custom_call_target="tpu_custom_call" | custom-call | tf_op jit(solution)/shard_map/fno_backward/pallas_call | solution.py:544
  98.1 0.0 copy-start
  98.1 3.2 %copy.26 = f32[1,32,8,16,128]{4,3,2,1,0:T(8,128)} copy(f32[1,32,8,16,128]{4,3,2,1,0:T(8,128)} %bitcast.3) | data formatting | bytes 4194304
  101.3 0.0 copy-done
  101.3 0.7 copy.27
Async XLA Ops:
  98.1 3.2 %copy-start = (f32[8,8192]{1,0:T(8,128)S(1)}, f32[8,8192]{1,0:T(8,128)}, u32[]{:S(2)}) copy-start(f32[8,8192]{1,0:T(8,128)} %get-tuple-element.9) | copy-start | bytes 786436

commit v2 on v1

--- a/solution.py
+++ b/solution.py
@@ -332,8 +332,6 @@
             total = term if total is None else total + term
         out2[n] = total.reshape(16, 16, 128)
         over_ring(out2.at[n], recv2.at[n], 6 * n + 2)
-        if n == 0:
-            spread_weights()
         arrived(recv2.at[n], 6 * n + 2)
         v = left3(yfh[...], yfl[...], recv2[n].reshape(256, 128)) * scale
         return jnp.concatenate(pack_kz(v), axis=0)
@@ -427,13 +425,14 @@
     depth_forward(field, 1 - zl, out1.at[0])
     pl.when(on_self)(lambda: pl.semaphore_wait(barrier, 31))
     pl.when(jnp.logical_not(on_self))(lambda: pl.semaphore_wait(barrier, 33))
+    move_weights()
     send_half(0, False)
     depth_forward(field, zl, out1.at[0])
     send_half(0, True)
-    move_weights()
     for k in range(2, n_tab):
         fetch(k).wait()
     kron(False)
+    spread_weights()
     pointwise(field, local)
 
     operands = right2(middle_forward(0, scale_cells), use[...])
@@ -442,15 +441,17 @@
     wait_weights()
 
     def mix(pair, total):
-        cols = pl.ds(pl.multiple_of(pair * 128, 128), 128)
+        cols = pl.ds(pair * 128, 128)
         tiles = [wloc[j, :, :, cols].reshape(32, 128) for j in range(4)]
         both = [
             jnp.concatenate([use_ref[b, j] * tiles[j] for j in range(4)], axis=0) for b in range(2)
         ]
-        rows = pl.ds(pl.multiple_of(pair * 256, 256), 256)
+        rows = pl.ds(pair * 256, 256)
         return total + right2(jnp.concatenate(both, axis=1), gather[rows])
 
-    mixed = lax.fori_loop(0, 16, mix, jnp.zeros((128, 128), F32))
+    mixed = jnp.zeros((128, 128), F32)
+    for pair in range(16):
+        mixed = mix(pair, mixed)
     send_back(mixed, 0, scale_modes)
     middle_inverse(0)
 
@@ -472,9 +473,9 @@
 
     def adjoint(pair, carry):
         first, second = carry
-        cols = pl.ds(pl.multiple_of(pair * 256, 256), 256)
+        cols = pl.ds(pair * 256, 256)
         wide = dot(spec_high, spread[:, cols]) + dot(spec_low, spread[:, cols])
-        cols = pl.ds(pl.multiple_of(pair * 128, 128), 128)
+        cols = pl.ds(pair * 128, 128)
         ones, twos = [], []
         for j in range(4):
             zr = wide[j * 32 : (j + 1) * 32, :128]
@@ -485,25 +486,24 @@
             gloc[j, :, :, cols] = (zr * use_ref[0, j] + zi * use_ref[1, j]).reshape(4, 8, 128)
         return first + jnp.concatenate(ones, axis=0), second + jnp.concatenate(twos, axis=0)
 
-    zero = jnp.zeros((128, 128), F32)
-    both = jnp.concatenate(lax.fori_loop(0, 16, adjoint, (zero, zero)), axis=1)
+    sums = (jnp.zeros((128, 128), F32),) * 2
+    for pair in range(16):
+        sums = adjoint(pair, sums)
+    both = jnp.concatenate(sums, axis=1)
     send_back(right2(both, fold[...]), 1, scale_cells)
-    for k in (2, 1, 3):
-        to = (s + k) % 4
-        push(gloc.at[to], grecv.at[k - 1], 14, 14, (to, gx, h))
+    for part in range(4):
+        for k in (2, 1, 3):
+            to = (s + k) % 4
+            push(gloc.at[to, part], grecv.at[part, k - 1], 14, 16 + part, (to, gx, h))
     middle_inverse(1)
 
-    arrived(grecv, 14)
-    for k in range(4):
-        gsum[k] = (gloc[s, k] + grecv[0, k]) + (grecv[1, k] + grecv[2, k])
-
-    def return_sum(k):
-        push(gsum.at[k], gspec.at[:, weight_cols(yp)], 15, 15, owner(k))
-
-    for k in range(1, 4):
-        return_sum((h + k) % 4)
-    pl.when(on_self)(lambda: keep(gsum.at[h % 4], gspec.at[:, weight_cols(yp)], 15))
-    pl.when(jnp.logical_not(on_self))(lambda: return_sum(h % 4))
+    for part in range(4):
+        arrived(grecv.at[part], 16 + part)
+        gsum[part] = (gloc[s, part] + grecv[part, 0]) + (grecv[part, 1] + grecv[part, 2])
+        own = jnp.logical_and(on_self, h % 4 == part)
+        target = gspec.at[:, weight_cols(yp)]
+        pl.when(own)(lambda: keep(gsum.at[part], target, 15))
+        pl.when(jnp.logical_not(own))(lambda: push(gsum.at[part], target, 15, 15, owner(part)))
 
     def finish(c, half, value):
         grad[c, :, half] = value + local[c, :, half]
@@ -562,7 +562,7 @@
             pltpu.VMEM((8, 8192), F32),
             pltpu.VMEM(rows, F32),
             pltpu.VMEM(rows, F32),
-            pltpu.VMEM((3,) + rows[1:], F32),
+            pltpu.VMEM((4, 3, 8, 2048), F32),
             pltpu.VMEM(rows[1:], F32),
             pltpu.VMEM((2, 256, 256), BF16),
             pltpu.VMEM((2, 4, 32, 128), F32),
@@ -578,7 +578,7 @@
             pltpu.SemaphoreType.DMA((len(TABLES),)),
             pltpu.SemaphoreType.DMA((2,)),
             pltpu.SemaphoreType.DMA((16,)),
-            pltpu.SemaphoreType.DMA((16,)),
+            pltpu.SemaphoreType.DMA((20,)),
         ],
         compiler_params=pltpu.CompilerParams(
             has_side_effects=True, collective_id=0, vmem_limit_bytes=63 * 1024 * 1024

time: 103 us -> 96.1 us (0.933)
  Pallas kernels: 97.4 us -> 91.4 us
    pallas_call x1, Pallas kernels: 97.4 us -> 91.4 us  [body(): pl.pallas_call(kernel, out_shape=(jax.ShapeDtypeStruct(shape, F32), jax.S...]
where the time goes in v2:
time: 96.1 us; the launch traced here: 95.9 us
  Pallas kernels  91.4 us (95%)
  local copies, waits for them, and re-layouts  3.88 us (4%)
    pallas_call x1, Pallas kernels, body(): pl.pallas_call(kernel, out_shape=(jax.ShapeDtypeStruct(shape, F32), jax.S...  91.4 us
    unnamed x4, local copies, waits for them, and re-layouts  3.88 us

profile of v2, /device:TPU:1, one launch (start us, length us, event | category | flops | bytes accessed | tf_op | source)
XLA Modules:
  0.0 95.9 jit_solution(10976517783165256145)
XLA Ops:
  0.6 91.4 %fno_backward.1 = (f32[32,8,2,8,128]{4,3,2,1,0:T(8,128)}, f32[8,8192]{1,0:T(8,128)}) custom-call(f32[32,8,2,8,128]{4,3,2,1,0:T(8,128)} %bitcast.4, f32[32,8,2,8,128]{4,3,2,1,0:T(8,128)} %bitcast.5, f32[8,8192]{1,0:T(8,128)} %weight_hbm.1, f32[32,32]{1,0:T(8,128)} %point_ref.1, f32[32]{0:T(128)} %bias_ref.1, bf16[1024,256]{1,0:T(8,128)(2,1)} %constant.34.clone.rest_0_, ...), custom_call_target="tpu_custom_call" | custom-call | tf_op jit(solution)/shard_map/fno_backward/pallas_call | solution.py:544
  92.0 0.0 copy-start
  92.0 3.2 %copy.26 = f32[1,32,8,16,128]{4,3,2,1,0:T(8,128)} copy(f32[1,32,8,16,128]{4,3,2,1,0:T(8,128)} %bitcast.3) | data formatting | bytes 4194304
  95.2 0.0 copy-done
  95.2 0.7 copy.27
Async XLA Ops:
  92.0 3.2 %copy-start = (f32[8,8192]{1,0:T(8,128)S(1)}, f32[8,8192]{1,0:T(8,128)}, u32[]{:S(2)}) copy-start(f32[8,8192]{1,0:T(8,128)} %get-tuple-element.9) | copy-start | bytes 786436

commit v3 on v2

--- a/solution.py
+++ b/solution.py
@@ -21,6 +21,8 @@
 MESH = pl.DeviceIdType.MESH
 
 KX = np.array([4 * ((d // 2) % 4) + 2 * (d % 2) + d // 8 for d in range(16)])
+
+FAR_FIRST = (8, 7, 9, 6, 10, 5, 11, 4, 12, 3, 13, 2, 14, 1, 15)
 
 
 def cos_sin(count, freqs):
@@ -81,8 +83,10 @@
         fold[0, :, i, 1, C + i] = -1.0
     rows8 = np.repeat(np.eye(C), 8, axis=0)
     out = []
-    for t in (z_fwd, x_fwd, y_fwd, y_inv, x_inv, z_inv):
+    for t in (z_fwd, z_inv):
         out += halves(t)
+    for t in (x_fwd, y_fwd, y_inv, x_inv):
+        out.append(np.concatenate(halves(t), axis=-2))
     out += [
         t.astype(jnp.bfloat16)
         for t in (
@@ -113,19 +117,23 @@
     return jnp.dot(a, b, preferred_element_type=F32)
 
 
-def left3(high, low, x):
+def left3(table, x):
+    half = table.shape[0] // 2
+    y = dot(table, jnp.concatenate(split(x), axis=1))
+    return y[:half, :128] + (y[half:, :128] + y[:half, 128:])
+
+
+def right2(x, table):
+    half = x.shape[0]
+    y = dot(jnp.concatenate(split(x), axis=0), table)
+    return y[:half] + y[half:]
+
+
+def right3(x, high, low):
+    half = x.shape[0]
     xh, xl = split(x)
-    return dot(high, xh) + (dot(low, xh) + dot(high, xl))
-
-
-def right3(x, high, low):
-    xh, xl = split(x)
-    return dot(xh, high) + (dot(xl, high) + dot(xh, low))
-
-
-def right2(x, table):
-    xh, xl = split(x)
-    return dot(xh, table) + dot(xl, table)
+    y = dot(jnp.concatenate([xh, xl], axis=0), high)
+    return y[:half] + (y[half:] + dot(xh, low))
 
 
 def lanes_of(rows):
@@ -208,7 +216,7 @@
         send_sem,
         recv_sem,
     ) = scratch[n_tab:]
-    (zfh, zfl, xfh, xfl, yfh, yfl, yih, yil, xih, xil, zih, zil, use, spread, gather, fold, rows8) = tab
+    (zfh, zfl, zih, zil, xf, yf, yi, xi, use, spread, gather, fold, rows8) = tab
 
     s = lax.axis_index("dp")
     gx = lax.axis_index("gx")
@@ -231,7 +239,7 @@
     def hello(device):
         pl.semaphore_signal(barrier, inc=1, device_id=device, device_id_type=MESH)
 
-    for k in range(1, 16):
+    for k in FAR_FIRST:
         to = (place + k) % 16
         hello((s, 2 * yp + to % 2, to // 2))
     for k in range(1, 8):
@@ -290,7 +298,7 @@
         keep(src.at[block], dst.at[block], stage + zl)
 
     def over_ring(src, dst, stage):
-        for k in (8, 7, 9, 6, 10, 5, 11, 4, 12, 3, 13, 2, 14, 1, 15):
+        for k in FAR_FIRST:
             to = (place + k) % 16
             push(src.at[to], dst.at[place], stage, stage, (s, 2 * yp + to % 2, to // 2))
         keep(src.at[place], dst.at[place], stage)
@@ -328,27 +336,28 @@
         for half in (zl, 1 - zl):
             part = recv1.at[n, pl.ds(half * 4, 4)]
             arrived(part, 6 * n + half)
-            term = left3(xfh[half], xfl[half], part[...].reshape(512, 128))
+            term = left3(xf[half], part[...].reshape(512, 128))
             total = term if total is None else total + term
         out2[n] = total.reshape(16, 16, 128)
         over_ring(out2.at[n], recv2.at[n], 6 * n + 2)
         arrived(recv2.at[n], 6 * n + 2)
-        v = left3(yfh[...], yfl[...], recv2[n].reshape(256, 128)) * scale
+        v = left3(yf[...], recv2[n].reshape(256, 128)) * scale
         return jnp.concatenate(pack_kz(v), axis=0)
 
     def send_back(rows, n, scale):
         planes = unpack_kz([rows[j * 32 : (j + 1) * 32] * scale for j in range(4)])
-        out5[n] = left3(yih[...], yil[...], planes).reshape(16, 16, 128)
+        out5[n] = left3(yi[...], planes).reshape(16, 16, 128)
         over_ring(out5.at[n], recv5.at[n], 6 * n + 3)
 
     def middle_inverse(n):
         arrived(recv5.at[n], 6 * n + 3)
-        high, low = split(recv5[n].reshape(256, 128))
+        rows = jnp.concatenate(split(recv5[n].reshape(256, 128)), axis=1)
         for half_is_own in (False, True):
             half = zl if half_is_own else 1 - zl
             for dy in (2, 1, 3, 0):
                 block = half * 4 + (yp + dy) % 4
-                value = dot(xih[block], high) + (dot(xil[block], high) + dot(xih[block], low))
+                value = dot(xi[block], rows)
+                value = value[:128, :128] + (value[128:, :128] + value[:128, 128:])
                 out6[n, block] = value.reshape(2, 8, 8, 128)
                 if half_is_own and dy == 0:
                     keep_gx(out6.at[n], recv6.at[n], 6 * n + 4)
@@ -363,10 +372,9 @@
         rows = jnp.concatenate(
             [jnp.concatenate([parts[0][cg], parts[1][cg]], axis=1) for cg in range(4)], axis=0
         )
-        high, low = split(rows)
         for pair in range(4):
             cols = pl.ds(pair * 256, 256)
-            value = dot(high, zih[:, cols]) + (dot(low, zih[:, cols]) + dot(high, zil[:, cols]))
+            value = right3(rows, zih[:, cols], zil[:, cols])
             for cg in range(4):
                 for k in range(2):
                     finish(
@@ -390,7 +398,8 @@
     def pointwise(src, dst):
         def one(x, carry):
             block = jnp.concatenate([src[:, x, yh].reshape(256, 128) for yh in range(2)], axis=1)
-            value = left3(point_kron[0], point_kron[1], block)
+            high, low = split(block)
+            value = dot(point_kron[0], high) + (dot(point_kron[1], high) + dot(point_kron[0], low))
             for yh in range(2):
                 dst[:, x, yh] = value[:, yh * 128 : (yh + 1) * 128].reshape(32, 8, 128)
             return carry
@@ -404,17 +413,19 @@
         inputs[1].wait()
 
         def one(k):
-            push(weight.at[:, weight_cols(k)], wloc.at[s, h % 4], 12, 12, mover(k))
+            push(weight.at[:, weight_cols(k)], wloc.at[s, h % 4], 12, 20 + h % 4, mover(k))
 
         for k in range(1, 4):
             one((yp + k) % 4)
-        pl.when(on_self)(lambda: keep(weight.at[:, weight_cols(yp)], wloc.at[s, h % 4], 12))
+        pl.when(on_self)(lambda: keep(weight.at[:, weight_cols(yp)], wloc.at[s, h % 4], 20 + h % 4))
         pl.when(jnp.logical_not(on_self))(lambda: one(yp))
 
     def spread_weights():
-        arrived(wloc.at[s], 12)
-        for k in (2, 1, 3):
-            push(wloc.at[s], wloc.at[s], 13, 13, ((s + k) % 4, gx, h))
+        for part in (h % 4, (h // 2 % 2) * 2 + 1 - h % 2, (1 - h // 2 % 2) * 2 + h % 2, 3 - h % 4):
+            block = wloc.at[s, part]
+            arrived(block, 20 + part)
+            for k in (2, 1, 3):
+                push(block, block, 13, 13, ((s + k) % 4, gx, h))
 
     def wait_weights():
         arrived(wloc.at[pl.ds(0, 3)], 13)
@@ -429,10 +440,10 @@
     send_half(0, False)
     depth_forward(field, zl, out1.at[0])
     send_half(0, True)
+    spread_weights()
     for k in range(2, n_tab):
         fetch(k).wait()
     kron(False)
-    spread_weights()
     pointwise(field, local)
 
     operands = right2(middle_forward(0, scale_cells), use[...])
@@ -469,12 +480,13 @@
     kron(True)
     pointwise(slope, local)
 
-    spec_high, spec_low = split(middle_forward(1, scale_modes))
+    spectra = jnp.concatenate(split(middle_forward(1, scale_modes)), axis=0)
 
     def adjoint(pair, carry):
         first, second = carry
         cols = pl.ds(pair * 256, 256)
-        wide = dot(spec_high, spread[:, cols]) + dot(spec_low, spread[:, cols])
+        wide = dot(spectra, spread[:, cols])
+        wide = wide[:128] + wide[128:]
         cols = pl.ds(pair * 128, 128)
         ones, twos = [], []
         for j in range(4):
@@ -533,6 +545,22 @@
 
     grad_out.wait()
     spec_out.wait()
+
+
+def hand_over(grad, gspec, grad_out, gspec_out, held, held_spec, in_sem, out_sem):
+    first = [pltpu.make_async_copy(gspec, held_spec, in_sem.at[8])]
+    second = [pltpu.make_async_copy(held_spec, gspec_out, out_sem.at[8])]
+    for k in range(8):
+        part = pl.ds(k * 4, 4)
+        first.append(pltpu.make_async_copy(grad.at[part], held.at[part], in_sem.at[k]))
+        second.append(pltpu.make_async_copy(held.at[part], grad_out.at[part], out_sem.at[k]))
+    for copy in first:
+        copy.start()
+    for k in range(9):
+        first[k].wait()
+        second[k].start()
+    for copy in second:
+        copy.wait()
 
 
 def body(field, cotangent, spectral_weight, pointwise_weight, bias):
@@ -578,7 +606,7 @@
             pltpu.SemaphoreType.DMA((len(TABLES),)),
             pltpu.SemaphoreType.DMA((2,)),
             pltpu.SemaphoreType.DMA((16,)),
-            pltpu.SemaphoreType.DMA((20,)),
+            pltpu.SemaphoreType.DMA((24,)),
         ],
         compiler_params=pltpu.CompilerParams(
             has_side_effects=True, collective_id=0, vmem_limit_bytes=63 * 1024 * 1024
@@ -592,6 +620,23 @@
         bias,
         *[jnp.asarray(t) for t in TABLES],
     )
+    grad_input, grad_spectral = pl.pallas_call(
+        hand_over,
+        out_shape=(
+            jax.ShapeDtypeStruct(shape, F32),
+            jax.ShapeDtypeStruct(spectral_weight.shape, F32),
+        ),
+        in_specs=[any_spec] * 2,
+        out_specs=(any_spec, any_spec),
+        scratch_shapes=[
+            pltpu.VMEM(shape, F32),
+            pltpu.VMEM(spectral_weight.shape, F32),
+            pltpu.SemaphoreType.DMA((9,)),
+            pltpu.SemaphoreType.DMA((9,)),
+        ],
+        compiler_params=pltpu.CompilerParams(vmem_limit_bytes=63 * 1024 * 1024),
+        name="hand_over",
+    )(grad_input, grad_spectral)
     return grad_input.reshape(field.shape), grad_spectral
 
 

time: 96.1 us -> 92.6 us (0.964)
  local copies, waits for them, and re-layouts: 3.88 us -> 0 us
    unnamed x4 -> x0, local copies, waits for them, and re-layouts: 3.88 us -> none
    pallas_call x0 -> x1, Pallas kernels: none -> 2.5 us  [body(): pl.pallas_call(hand_over, out_shape=(jax.ShapeDtypeStruct(shape, F32), ja...]
    pallas_call x1, Pallas kernels: 91.4 us -> 89 us  [body(): pl.pallas_call(kernel, out_shape=(jax.ShapeDtypeStruct(shape, F32), jax.S...]
where the time goes in v3:
time: 92.6 us; the launch traced here: 92.1 us
  Pallas kernels  91.5 us (99%)
    pallas_call x1, Pallas kernels, body(): pl.pallas_call(kernel, out_shape=(jax.ShapeDtypeStruct(shape, F32), jax.S...  89 us
    pallas_call x1, Pallas kernels, body(): pl.pallas_call(hand_over, out_shape=(jax.ShapeDtypeStruct(shape, F32), ja...  2.5 us

profile of v3, /device:TPU:1, one launch (start us, length us, event | category | flops | bytes accessed | tf_op | source)
XLA Modules:
  0.0 92.1 jit_solution(5021777436648866712)
XLA Ops:
  0.6 89.0 %fno_backward.1 = (f32[32,8,2,8,128]{4,3,2,1,0:T(8,128)}, f32[8,8192]{1,0:T(8,128)}) custom-call(f32[32,8,2,8,128]{4,3,2,1,0:T(8,128)} %bitcast.3, f32[32,8,2,8,128]{4,3,2,1,0:T(8,128)} %bitcast.4, f32[8,8192]{1,0:T(8,128)} %weight_hbm.1, f32[32,32]{1,0:T(8,128)} %point_ref.1, f32[32]{0:T(128)} %bias_ref.1, bf16[1024,256]{1,0:T(8,128)(2,1)} %constant.26.clone.rest_0_, ...), custom_call_target="tpu_custom_call" | custom-call | tf_op jit(solution)/shard_map/fno_backward/pallas_call | solution.py:572
  89.6 2.5 %hand_over.1 = (f32[32,8,2,8,128]{4,3,2,1,0:T(8,128)}, f32[8,8192]{1,0:T(8,128)}) custom-call(f32[32,8,2,8,128]{4,3,2,1,0:T(8,128)} %get-tuple-element.6.grad, f32[8,8192]{1,0:T(8,128)} %get-tuple-element.7.gspec), custom_call_target="tpu_custom_call" | custom-call | tf_op jit(solution)/shard_map/hand_over/pallas_call | solution.py:623

commit v4 on v3

--- a/solution.py
+++ b/solution.py
@@ -51,8 +51,7 @@
     def inverse(c, s):
         return np.stack([np.stack([c, s], -1), np.stack([-s, c], -1)], -2)
 
-    z_fwd = np.einsum("zkr,cd->czrkd", ztable, eye8).reshape(8 * NZ, 2 * MZ * 8)
-    z_inv = np.ascontiguousarray(z_fwd.T)
+    z_fwd = np.einsum("zjyr,cd->czyrjd", ztable.reshape(NZ, 4, 4, 2), np.eye(4)).reshape(4 * NZ, 128)
     fx = forward(cx, sx).reshape(8, 8, 16, 2, 2)
     fx = fx.reshape(4, 2, 8, 16, 2, 2)
     x_fwd = np.einsum("gzxdrq,yw->zdqygrxw", fx, eye8).reshape(2, 256, 512)
@@ -81,10 +80,18 @@
         fold[1, :, i, 1, i] = 1.0
         fold[1, :, i, 0, C + i] = 1.0
         fold[0, :, i, 1, C + i] = -1.0
+    pack = np.zeros((2, 8, 4, 4, 4, 128), np.float32)
+    for p in range(2):
+        for j in range(4):
+            for c in range(C):
+                pack[p, c // 4, j, c % 4, j, p * C + c] = 1.0
+    pack = pack.reshape(256, 512)
     rows8 = np.repeat(np.eye(C), 8, axis=0)
     out = []
-    for t in (z_fwd, z_inv):
-        out += halves(t)
+    high, low = halves(z_fwd)
+    out.append(np.concatenate([high, low], axis=1))
+    out.append(np.ascontiguousarray(np.concatenate([high, high], axis=1).T))
+    out.append(np.ascontiguousarray(low.T))
     for t in (x_fwd, y_fwd, y_inv, x_inv):
         out.append(np.concatenate(halves(t), axis=-2))
     out += [
@@ -95,6 +102,8 @@
             np.ascontiguousarray(spread.T),
             fold.reshape(256, 128),
             rows8,
+            pack,
+            np.ascontiguousarray(pack.T),
         )
     ]
     return out
@@ -129,13 +138,6 @@
     return y[:half] + y[half:]
 
 
-def right3(x, high, low):
-    half = x.shape[0]
-    xh, xl = split(x)
-    y = dot(jnp.concatenate([xh, xl], axis=0), high)
-    return y[:half] + (y[half:] + dot(xh, low))
-
-
 def lanes_of(rows):
     return lax.broadcasted_iota(jnp.int32, (rows, 128), 1)
 
@@ -146,33 +148,24 @@
 
 
 def swap_groups(blocks):
-    group = (lanes_of(64) % 32) // 8
-    out = []
-    for a in range(4):
-        total = blocks[a]
-        for b in range(4):
-            if b != a:
-                total = jnp.where(group == b, roll(blocks[b], (b - a) * 8), total)
-        out.append(total)
-    return out
-
-
-def pack_kz(v):
-    lane = lanes_of(32)
-    return [
-        jnp.where(lane < 32, roll(v[:32], -j * 32), roll(v[32:], 32 - j * 32)) for j in range(4)
-    ]
-
-
-def unpack_kz(blocks):
-    lane = lanes_of(32)
-    parts = []
-    for p in range(2):
-        total = jnp.zeros((32, 128), F32)
-        for j in range(4):
-            total = total + jnp.where(lane // 32 == j, roll(blocks[j], (j - p) * 32), 0.0)
-        parts.append(total)
-    return jnp.concatenate(parts, axis=0)
+    lane = lanes_of(64)
+    for bit in (4, 2, 1):
+        width = 16 * bit
+        low = lane % (2 * width) < width
+        out = [None] * 8
+        for a in range(8):
+            if a & bit:
+                continue
+            first, second = blocks[a], blocks[a + bit]
+            if bit == 4:
+                moved = roll(jnp.where(low, second, first), 64)
+                out[a] = jnp.where(low, first, moved)
+                out[a + bit] = jnp.where(low, moved, second)
+            else:
+                out[a] = jnp.where(low, first, roll(second, width))
+                out[a + bit] = jnp.where(low, roll(first, -width), second)
+        blocks = out
+    return blocks
 
 
 def kernel(
@@ -216,7 +209,7 @@
         send_sem,
         recv_sem,
     ) = scratch[n_tab:]
-    (zfh, zfl, zih, zil, xf, yf, yi, xi, use, spread, gather, fold, rows8) = tab
+    (zf, zi, zil, xf, yf, yi, xi, use, spread, gather, fold, rows8, pack, unpack) = tab
 
     s = lax.axis_index("dp")
     gx = lax.axis_index("gx")
@@ -262,10 +255,9 @@
         for k, (a, b) in enumerate(((field_hbm, field), (weight_hbm, weight), (cot_hbm, cot)))
     ]
     fetch(0).start()
-    fetch(1).start()
     inputs[0].start()
     inputs[1].start()
-    for k in range(2, n_tab):
+    for k in range(1, n_tab):
         fetch(k).start()
     inputs[2].start()
 
@@ -304,23 +296,18 @@
         keep(src.at[place], dst.at[place], stage)
 
     def depth_forward(grid, half, dst):
-        total = jnp.zeros((256, 256), F32)
-        for pair in range(4):
-            block = jnp.concatenate(
-                [
-                    jnp.concatenate(
-                        [grid[cg * 8 + pair * 2 + k, :, half].reshape(64, 128) for k in range(2)], axis=1
-                    )
-                    for cg in range(4)
-                ],
-                axis=0,
-            )
-            rows = pl.ds(pair * 256, 256)
-            total = total + right3(block, zfh[rows], zfl[rows])
-        for r in range(2):
-            blocks = [total[cg * 64 : (cg + 1) * 64, r * 128 : (r + 1) * 128] for cg in range(4)]
-            for k, block in enumerate(swap_groups(blocks)):
-                dst[half * 4 + k, r] = block.reshape(8, 8, 128)
+        rows = jnp.concatenate(
+            [
+                jnp.concatenate([grid[b * 4 + k, :, half].reshape(64, 128) for k in range(4)], axis=1)
+                for b in range(8)
+            ],
+            axis=0,
+        )
+        high, low = split(rows)
+        wide = dot(high, zf[...])
+        total = wide[:, :128] + (wide[:, 128:] + dot(low, zf[:, :128]))
+        for a, block in enumerate(swap_groups([total[b * 64 : (b + 1) * 64] for b in range(8)])):
+            dst[half * 4 + a // 2, a % 2] = block.reshape(8, 8, 128)
 
     def send_half(n, half_is_own):
         half = zl if half_is_own else 1 - zl
@@ -342,10 +329,13 @@
         over_ring(out2.at[n], recv2.at[n], 6 * n + 2)
         arrived(recv2.at[n], 6 * n + 2)
         v = left3(yf[...], recv2[n].reshape(256, 128)) * scale
-        return jnp.concatenate(pack_kz(v), axis=0)
+        v = right2(jnp.concatenate([v[:32], v[32:]], axis=1), pack[...])
+        return jnp.concatenate([v[:, j * 128 : (j + 1) * 128] for j in range(4)], axis=0)
 
     def send_back(rows, n, scale):
-        planes = unpack_kz([rows[j * 32 : (j + 1) * 32] * scale for j in range(4)])
+        flat = jnp.concatenate([rows[j * 32 : (j + 1) * 32] * scale for j in range(4)], axis=1)
+        flat = right2(flat, unpack[...])
+        planes = jnp.concatenate([flat[:, :128], flat[:, 128:]], axis=0)
         out5[n] = left3(yi[...], planes).reshape(16, 16, 128)
         over_ring(out5.at[n], recv5.at[n], 6 * n + 3)
 
@@ -366,21 +356,18 @@
 
     def depth_inverse(n, half, finish):
         arrived(recv6.at[n, pl.ds(half * 4, 4)], 6 * n + 4 + half)
-        parts = []
-        for r in range(2):
-            parts.append(swap_groups([recv6[n, half * 4 + k, r].reshape(64, 128) for k in range(4)]))
-        rows = jnp.concatenate(
-            [jnp.concatenate([parts[0][cg], parts[1][cg]], axis=1) for cg in range(4)], axis=0
-        )
-        for pair in range(4):
+        blocks = swap_groups([recv6[n, half * 4 + a // 2, a % 2].reshape(64, 128) for a in range(8)])
+        high, low = split(jnp.concatenate(blocks, axis=0))
+        both = jnp.concatenate([high, low], axis=1)
+        for pair in range(2):
             cols = pl.ds(pair * 256, 256)
-            value = right3(rows, zih[:, cols], zil[:, cols])
-            for cg in range(4):
+            value = dot(both, zi[:, cols]) + dot(high, zil[:, cols])
+            for b in range(8):
                 for k in range(2):
                     finish(
-                        cg * 8 + pair * 2 + k,
+                        b * 4 + pair * 2 + k,
                         half,
-                        value[cg * 64 : (cg + 1) * 64, k * 128 : (k + 1) * 128].reshape(8, 8, 128),
+                        value[b * 64 : (b + 1) * 64, k * 128 : (k + 1) * 128].reshape(8, 8, 128),
                     )
 
     def kron(transposed):
@@ -424,14 +411,13 @@
         for part in (h % 4, (h // 2 % 2) * 2 + 1 - h % 2, (1 - h // 2 % 2) * 2 + h % 2, 3 - h % 4):
             block = wloc.at[s, part]
             arrived(block, 20 + part)
-            for k in (2, 1, 3):
+            for k in (1, 3, 2):
                 push(block, block, 13, 13, ((s + k) % 4, gx, h))
 
     def wait_weights():
         arrived(wloc.at[pl.ds(0, 3)], 13)
 
     fetch(0).wait()
-    fetch(1).wait()
     inputs[0].wait()
     depth_forward(field, 1 - zl, out1.at[0])
     pl.when(on_self)(lambda: pl.semaphore_wait(barrier, 31))
@@ -441,7 +427,7 @@
     depth_forward(field, zl, out1.at[0])
     send_half(0, True)
     spread_weights()
-    for k in range(2, n_tab):
+    for k in range(1, n_tab):
         fetch(k).wait()
     kron(False)
     pointwise(field, local)
@@ -503,14 +489,16 @@
         sums = adjoint(pair, sums)
     both = jnp.concatenate(sums, axis=1)
     send_back(right2(both, fold[...]), 1, scale_cells)
-    for part in range(4):
+    for i in range(4):
+        part = (yp + i) % 4
         for k in (2, 1, 3):
             to = (s + k) % 4
-            push(gloc.at[to, part], grecv.at[part, k - 1], 14, 16 + part, (to, gx, h))
+            push(gloc.at[to, part], grecv.at[part, k - 1], 14, 16 + i, (to, gx, h))
     middle_inverse(1)
 
-    for part in range(4):
-        arrived(grecv.at[part], 16 + part)
+    for i in range(4):
+        part = (yp + i) % 4
+        arrived(grecv.at[part], 16 + i)
         gsum[part] = (gloc[s, part] + grecv[part, 0]) + (grecv[part, 1] + grecv[part, 2])
         own = jnp.logical_and(on_self, h % 4 == part)
         target = gspec.at[:, weight_cols(yp)]

time: 92.6 us -> 91.2 us (0.985)
  Pallas kernels: 91.5 us -> 89.5 us
    pallas_call x1, Pallas kernels: 89 us -> 87 us  [body(): pl.pallas_call(kernel, out_shape=(jax.ShapeDtypeStruct(shape, F32), jax.S...]
where the time goes in v4:
time: 91.2 us; the launch traced here: 90.1 us
  Pallas kernels  89.5 us (98%)
    pallas_call x1, Pallas kernels, body(): pl.pallas_call(kernel, out_shape=(jax.ShapeDtypeStruct(shape, F32), jax.S...  87 us
    pallas_call x1, Pallas kernels, body(): pl.pallas_call(hand_over, out_shape=(jax.ShapeDtypeStruct(shape, F32), ja...  2.5 us

profile of v4, /device:TPU:1, one launch (start us, length us, event | category | flops | bytes accessed | tf_op | source)
XLA Modules:
  0.0 90.1 jit_solution(1430638329878552909)
XLA Ops:
  0.6 87.0 %fno_backward.1 = (f32[32,8,2,8,128]{4,3,2,1,0:T(8,128)}, f32[8,8192]{1,0:T(8,128)}) custom-call(f32[32,8,2,8,128]{4,3,2,1,0:T(8,128)} %bitcast.3, f32[32,8,2,8,128]{4,3,2,1,0:T(8,128)} %bitcast.4, f32[8,8192]{1,0:T(8,128)} %weight_hbm.1, f32[32,32]{1,0:T(8,128)} %point_ref.1, f32[32]{0:T(128)} %bias_ref.1, bf16[512,256]{1,0:T(8,128)(2,1)} %constant.28.clone.rest_0_, ...), custom_call_target="tpu_custom_call" | custom-call | tf_op jit(solution)/shard_map/fno_backward/pallas_call | solution.py:560
  87.6 2.5 %hand_over.1 = (f32[32,8,2,8,128]{4,3,2,1,0:T(8,128)}, f32[8,8192]{1,0:T(8,128)}) custom-call(f32[32,8,2,8,128]{4,3,2,1,0:T(8,128)} %get-tuple-element.6.grad, f32[8,8192]{1,0:T(8,128)} %get-tuple-element.7.gspec), custom_call_target="tpu_custom_call" | custom-call | tf_op jit(solution)/shard_map/hand_over/pallas_call | solution.py:611

commit v5 on v4

--- a/solution.py
+++ b/solution.py
@@ -382,7 +382,7 @@
             )
             point_kron[k] = jnp.where(same, wide, 0.0).astype(BF16)
 
-    def pointwise(src, dst):
+    def pointwise(src, dst, first, last):
         def one(x, carry):
             block = jnp.concatenate([src[:, x, yh].reshape(256, 128) for yh in range(2)], axis=1)
             high, low = split(block)
@@ -391,7 +391,7 @@
                 dst[:, x, yh] = value[:, yh * 128 : (yh + 1) * 128].reshape(32, 8, 128)
             return carry
 
-        lax.fori_loop(0, 8, one, 0)
+        lax.fori_loop(first, last, one, 0)
 
     def weight_cols(k):
         return pl.ds(pl.multiple_of(k * 2048, 2048), 2048)
@@ -407,8 +407,8 @@
         pl.when(on_self)(lambda: keep(weight.at[:, weight_cols(yp)], wloc.at[s, h % 4], 20 + h % 4))
         pl.when(jnp.logical_not(on_self))(lambda: one(yp))
 
-    def spread_weights():
-        for part in (h % 4, (h // 2 % 2) * 2 + 1 - h % 2, (1 - h // 2 % 2) * 2 + h % 2, 3 - h % 4):
+    def spread_weights(parts):
+        for part in parts:
             block = wloc.at[s, part]
             arrived(block, 20 + part)
             for k in (1, 3, 2):
@@ -422,15 +422,17 @@
     depth_forward(field, 1 - zl, out1.at[0])
     pl.when(on_self)(lambda: pl.semaphore_wait(barrier, 31))
     pl.when(jnp.logical_not(on_self))(lambda: pl.semaphore_wait(barrier, 33))
+    send_half(0, False)
     move_weights()
-    send_half(0, False)
     depth_forward(field, zl, out1.at[0])
     send_half(0, True)
-    spread_weights()
     for k in range(1, n_tab):
         fetch(k).wait()
     kron(False)
-    pointwise(field, local)
+    spread_weights((h % 4, (h // 2 % 2) * 2 + 1 - h % 2))
+    pointwise(field, local, 0, 4)
+    spread_weights(((1 - h // 2 % 2) * 2 + h % 2, 3 - h % 4))
+    pointwise(field, local, 4, 8)
 
     operands = right2(middle_forward(0, scale_cells), use[...])
     for b in range(2):
@@ -464,7 +466,7 @@
         depth_forward(slope, half, out1.at[1])
         send_half(1, half_is_own)
     kron(True)
-    pointwise(slope, local)
+    pointwise(slope, local, 0, 8)
 
     spectra = jnp.concatenate(split(middle_forward(1, scale_modes)), axis=0)
 
@@ -491,7 +493,7 @@
     send_back(right2(both, fold[...]), 1, scale_cells)
     for i in range(4):
         part = (yp + i) % 4
-        for k in (2, 1, 3):
+        for k in (1, 3, 2):
             to = (s + k) % 4
             push(gloc.at[to, part], grecv.at[part, k - 1], 14, 16 + i, (to, gx, h))
     middle_inverse(1)

time: 91.2 us -> 89.3 us (0.979)
  Pallas kernels: 89.5 us -> 88.4 us
    pallas_call x1, Pallas kernels: 87 us -> 85.9 us  [body(): pl.pallas_call(kernel, out_shape=(jax.ShapeDtypeStruct(shape, F32), jax.S...]
where the time goes in v5:
time: 89.3 us; the launch traced here: 89.1 us
  Pallas kernels  88.4 us (99%)
    pallas_call x1, Pallas kernels, body(): pl.pallas_call(kernel, out_shape=(jax.ShapeDtypeStruct(shape, F32), jax.S...  85.9 us
    pallas_call x1, Pallas kernels, body(): pl.pallas_call(hand_over, out_shape=(jax.ShapeDtypeStruct(shape, F32), ja...  2.5 us

profile of v5, /device:TPU:1, one launch (start us, length us, event | category | flops | bytes accessed | tf_op | source)
XLA Modules:
  0.0 89.1 jit_solution(1643461186022353633)
XLA Ops:
  0.6 85.9 %fno_backward.1 = (f32[32,8,2,8,128]{4,3,2,1,0:T(8,128)}, f32[8,8192]{1,0:T(8,128)}) custom-call(f32[32,8,2,8,128]{4,3,2,1,0:T(8,128)} %bitcast.3, f32[32,8,2,8,128]{4,3,2,1,0:T(8,128)} %bitcast.4, f32[8,8192]{1,0:T(8,128)} %weight_hbm.1, f32[32,32]{1,0:T(8,128)} %point_ref.1, f32[32]{0:T(128)} %bias_ref.1, bf16[512,256]{1,0:T(8,128)(2,1)} %constant.28.clone.rest_0_, ...), custom_call_target="tpu_custom_call" | custom-call | tf_op jit(solution)/shard_map/fno_backward/pallas_call | solution.py:562
  86.6 2.5 %hand_over.1 = (f32[32,8,2,8,128]{4,3,2,1,0:T(8,128)}, f32[8,8192]{1,0:T(8,128)}) custom-call(f32[32,8,2,8,128]{4,3,2,1,0:T(8,128)} %get-tuple-element.6.grad, f32[8,8192]{1,0:T(8,128)} %get-tuple-element.7.gspec), custom_call_target="tpu_custom_call" | custom-call | tf_op jit(solution)/shard_map/hand_over/pallas_call | solution.py:613
